TPU v7x, 32 devices: a whole 2x2x4 slice. The times are simulated.
32 devices in a mesh: groups: 2 (over x), ctx: 16 (over z, y, core).
Axes of the slice: x: 2, y: 2, z: 4, core: 2. Of those that a mesh axis runs over, the one named last changes fastest.
Arguments:
- hidden: bfloat16 [24576, 4096], P(('groups', 'ctx')), parts along dimension 0, may hold values from -6 to 6
- w_qkv: bfloat16 [4096, 768], P('ctx'), may hold values from -0.09375 to 0.09375
- w_out: bfloat16 [256, 4096], P('ctx'), may hold values from -0.375 to 0.375
- norm_gain: float32 [256], replicated, may hold values from 0.1 to 1.9
- incoming: float32 [4, 128, 128], P('groups'), parts along dimension 0, may hold values from -600 to 600
Outputs:
- attn_out: bfloat16 [24576, 4096], P(('groups', 'ctx')), parts along dimension 0
There are 2 independent parts, one for each index of `groups`. A program takes and returns all parts, laid end to end along the dimension named above; an argument that names none is the same for every part. Nothing has to cross between parts.
All inputs are finite; a program needn't handle non-finite values.
Results may differ from a plain program's by a relative error of at most 0.0065.
Values may be sent and summed in bfloat16 or wider, within the bound.
A program may use at most 64 MiB of HBM per device.

v0:
```python
import jax
import jax.numpy as jnp
from jax import lax
from jax.sharding import PartitionSpec as P


def carried_in(value, axis, join, neutral):
    count, mine = (lax.axis_size(axis), lax.axis_index(axis))
    pieces = lax.all_gather(value, axis)
    running = jnp.full_like(value, 0) + jnp.asarray(neutral, value.dtype)

    def turn(position, running):
        longer = join(running, pieces[position])
        return jnp.where(position < mine, longer, running)

    return lax.fori_loop(0, count - 1, turn, running)


def local(hidden, w_qkv, w_out, norm_gain, incoming):
    tokens_here = hidden.shape[0]
    width = w_qkv.shape[1] // 3
    heads = incoming.shape[0]
    head_size = incoming.shape[1]
    columns = hidden
    proj = jnp.dot(
        columns,
        lax.all_gather(w_qkv, "ctx", axis=0, tiled=True),
        preferred_element_type=jnp.float32,
    ).astype(jnp.bfloat16)
    query = proj[:, :width].reshape(tokens_here, heads, head_size)
    keys = proj[:, width : 2 * width].reshape(tokens_here, heads, head_size)
    values = proj[:, 2 * width :].reshape(tokens_here, heads, head_size)
    state = jnp.einsum("thd,the->hde", keys, values, preferred_element_type=jnp.float32)
    zero_state = jnp.zeros_like(state)

    def add_states(earlier, later):
        return earlier + later

    before = carried_in(state, "ctx", add_states, zero_state)
    prior = incoming + before
    scores = jnp.einsum("thd,shd->hts", query, keys, preferred_element_type=jnp.float32)
    rows = jnp.arange(tokens_here)
    causal = rows[:, None] >= rows[None, :]
    scores = jnp.where(causal[None], scores, 0.0).astype(jnp.bfloat16)
    intra = jnp.einsum("hts,she->the", scores, values, preferred_element_type=jnp.float32)
    cross = jnp.einsum(
        "thd,hde->the", query.astype(jnp.float32), prior, precision=lax.Precision.HIGHEST
    )
    mixed = intra + cross
    scale = lax.rsqrt(jnp.mean(mixed * mixed, axis=-1, keepdims=True) + 1e-06)
    gains = norm_gain.reshape(heads, head_size)
    normed = (mixed * scale * gains).astype(jnp.bfloat16).reshape(tokens_here, width)
    columns = normed
    result = jnp.dot(
        columns,
        lax.all_gather(w_out, "ctx", axis=0, tiled=True),
        preferred_element_type=jnp.float32,
    )
    return result.astype(jnp.bfloat16)


def solution(mesh):
    return jax.shard_map(
        local,
        mesh=mesh,
        in_specs=(
            P(("groups", "ctx"), None),
            P("ctx", None),
            P("ctx", None),
            P(),
            P("groups", None, None),
        ),
        out_specs=P(("groups", "ctx"), None),
        check_vma=False,
    )
```

profile of v0, /device:TPU:0, one launch (start us, length us, event | category | flops | bytes accessed | tf_op | source)
XLA Modules:
  0.0 179.5 jit_solution(12376154910145856354)
XLA Ops:
  6.5 0.7 all-gather.5.cloned.1.call-update
  7.3 66.9 %all-gather.5.cloned.1.call-done = bf16[4096,768]{1,0:T(8,128)(2,1)} async-done(((bf16[256,768]{1,0:T(8,128)(2,1)}), bf16[4096,768]{1,0:T(8,128)(2,1)}) %all-gather.5.cloned.1.call-update) | async-done | bytes 6291472 | tf_op jit(solution)/shard_map/all_gather | solution.py:27
  74.2 9.1 %convolution_convert_fusion.1 = bf16[768,768]{0,1:T(8,128)(2,1)S(1)} fusion(bf16[768,4096]{1,0:T(8,128)(2,1)} %param.7, bf16[4096,768]{1,0:T(8,128)(2,1)} %all-gather.5.cloned.1.call-done), kind=kOutput, calls=%fused_computation.8 | convolution fusion | flops 4832428032 | bytes 13762560 | tf_op jit(solution)/shard_map/dot_general | solution.py:25
  83.4 0.9 fusion.11
  85.3 39.2 %all-gather.9.cloned.1.call-done = f32[32,128,128]{2,1,0:T(8,128)} async-done(((f32[2,128,128]{2,1,0:T(8,128)}), f32[32,128,128]{2,1,0:T(8,128)}) %all-gather.9.cloned.1.call-update) | async-done | bytes 2097168 | tf_op jit(solution)/shard_map/all_gather | solution.py:9
  124.5 14.6 %while.14 = (s32[]{:T(128)}, f32[2,128,128]{2,1,0:T(8,128)S(1)}, s32[]{:T(128)}, f32[16,2,128,128]{3,2,1,0:T(8,128)}, s32[]{:T(128)}, /*index=5*/s32[]{:T(128)}) while((s32[]{:T(128)}, f32[2,128,128]{2,1,0:T(8,128)S(1)}, s32[]{:T(128)}, f32[16,2,128,128]{3,2,1,0:T(8,128)}, s32[]{:T(128)}, /*index=5*/s32[]{:T(128)}) %tuple.44), condition=%wide.region_1.2_spmd.clone, body=%wide.region_0.1_spmd.clone.sunk | while | flops 98308 | bytes 393317 | solution.py:16
  124.5 0.9 add_select_fusion.2
  125.5 0.9 add_select_fusion.2
  126.4 0.9 add_select_fusion.2
  127.4 0.9 add_select_fusion.2
  128.4 0.9 add_select_fusion.2
  129.4 0.9 add_select_fusion.2
  130.3 0.9 add_select_fusion.2
  131.3 0.9 add_select_fusion.2
  132.3 1.0 add_select_fusion.2
  133.3 1.0 add_select_fusion.2
  134.2 0.9 add_select_fusion.2
  135.2 0.9 add_select_fusion.2
  136.2 0.9 add_select_fusion.2
  137.2 0.9 add_select_fusion.2
  138.1 1.0 add_select_fusion.2
  139.7 1.6 multiply_reduce_fusion
  141.4 25.4 %all-gather.7.cloned.1.call-done = bf16[256,4096]{1,0:T(8,128)(2,1)} async-done(((bf16[16,4096]{1,0:T(8,128)(2,1)}), bf16[256,4096]{1,0:T(8,128)(2,1)}) %all-gather.7.cloned.1.call-update) | async-done | bytes 2097168 | tf_op jit(solution)/shard_map/all_gather | solution.py:56
  166.8 6.1 %convolution_convert_fusion = bf16[768,4096]{1,0:T(8,128)(2,1)} fusion(bf16[768,256]{0,1:T(8,128)(2,1)S(1)} %bitcast.22, bf16[256,4096]{1,0:T(8,128)(2,1)} %all-gather.7.cloned.1.call-done), kind=kOutput, calls=%fused_computation.1 | convolution fusion | flops 1613758464 | bytes 8781824 | tf_op jit(solution)/shard_map/dot_general | solution.py:54
  (15 shorter events, 1.7 us)
Async XLA Ops:
  6.5 67.7 %all-gather.5.cloned.1.call-start = ((), (), s32[]{:S(2)}) async-start(), calls=%async_computation | async-start | bytes 6684672 | tf_op jit(solution)/shard_map/all_gather | solution.py:27
  7.3 117.2 %all-gather.9.cloned.1.call-start = ((), (), s32[]{:S(2)}) async-start(), calls=%async_computation.2 | async-start | bytes 2228224 | tf_op jit(solution)/shard_map/all_gather | solution.py:9
  83.4 55.7 %copy-start = (f32[2,128,128]{2,1,0:T(8,128)S(1)}, f32[2,128,128]{2,1,0:T(8,128)}, u32[]{:S(2)}) copy-start(f32[2,128,128]{2,1,0:T(8,128)} %param.11) | copy-start | bytes 393220
  84.3 82.5 %all-gather.7.cloned.1.call-start = ((), (), s32[]{:S(2)}) async-start(), calls=%async_computation.1 | async-start | bytes 2228224 | tf_op jit(solution)/shard_map/all_gather | solution.py:56
  139.6 1.7 copy-start.1
Sparse Core Ops, SparseCore 0:
  9.6 64.5 all-gather.4
  84.5 39.9 all-gather.8
  126.7 40.0 all-gather.6
where the time goes:
time: 180 us; the launch traced here: 179 us
  waiting for transfers between devices  133 us (74%)
  matrix products  18.3 us (10%)
  other arithmetic  14.6 us (8%)
  between operations  13.2 us (7%)
    all_gather x1, waiting for transfers between devices, local(): lax.all_gather(w_qkv, 'ctx', axis=0, tiled=True)  66.9 us
    all_gather x1, waiting for transfers between devices, carried_in(): pieces = lax.all_gather(value, axis)  39.2 us
    all_gather x1, waiting for transfers between devices, local(): lax.all_gather(w_out, 'ctx', axis=0, tiled=True)  25.4 us
    select_n x15, other arithmetic, turn(): return jnp.where(position < mine, longer, running)  14.3 us
    dot_general x1, matrix products, local(): jnp.dot(columns, lax.all_gather(w_qkv, 'ctx', axis=0, tiled=True), prefer...  9.06 us
    dot_general x1, matrix products, local(): jnp.dot(columns, lax.all_gather(w_out, 'ctx', axis=0, tiled=True), prefer...  6.12 us
  transfers between devices with their start and end apart: 3, of which 3 were waited for; matrix products, arithmetic and copies ran while one was open for 9% of the time, Pallas kernels for 0%

commit v1 on v0

v1 whole, which is shorter than its diff:
```python
import functools

import jax
import jax.numpy as jnp
from jax import lax
from jax.experimental import pallas as pl
from jax.experimental.pallas import tpu as pltpu
from jax.sharding import PartitionSpec as P

MESH = pl.DeviceIdType.MESH
CORES = 2
RIGHT, LEFT = 0, 1


def bands(units, first):
    third = units * 5 // 16 if first else -(-units * 5 // 16)
    return third, units - 2 * third


def kernel(
    n_groups, n_ctx, heads, head_size, rows, o_cols,
    hid_hbm, wq_hbm, wo_hbm, gain_ref, inc_ref,
    normed_ref, wo_all,
    hid, wq, acc, proj, st_mine, st_peer, st_out, st_in, st_half, st_other,
    load_sem, ring_send, ring_recv, x_send, x_recv, sa_send, sa_recv, sb_send, sb_recv,
    own_send, own_recv, t_send, t_recv, p_send, p_recv,
):
    n = n_ctx // CORES
    half = n // 2
    snake = 2 if n == 8 else 1
    tokens = hid.shape[0]
    width = heads * head_size
    group = lax.axis_index("groups")
    ctx = lax.axis_index("ctx")
    core = lax.rem(ctx, CORES)
    chip = ctx // CORES
    side = lax.rem(group, 2)
    partner = (group + 1 - 2 * side, ctx)
    peer_ctx = ctx + 1 - 2 * core
    peer = (group, peer_ctx)

    def fold(k):
        if snake == 1:
            return k
        y = lax.rem(k, 2)
        z = k // 2
        return z + y * (n - 1 - 2 * z)

    def unfold(p):
        if snake == 1:
            return p
        y = p // (n // 2)
        z = p + y * (n - 1 - 2 * p)
        return z * 2 + y

    place = fold(chip)

    def chip_at(delta):
        return unfold(lax.rem(place + delta + 2 * n, n))

    to_right = (group, chip_at(1) * CORES + core)
    to_left = (group, chip_at(-1) * CORES + core)

    streams = []
    q_units = rows // 16 // 2
    o_units = o_cols // 128 // 2
    for u in range(2):
        b, a = bands(q_units, u == 0)
        streams.append((0, u * q_units * 16, b * 16, a * 16))
    for u in range(2):
        b, a = bands(o_units, u == 0)
        streams.append((1, u * o_units * 128, b * 128, a * 128))
    use_x = n_groups % 2 == 0
    if not use_x:
        streams = [(k, base, 0, 2 * b + a) for k, base, b, a in streams]
    hops = [(half, n - 1 - half), (n - 1 - half, half)] * 2

    def part(kind, dev, start, size):
        if kind == 0:
            at = pl.multiple_of(dev * rows + start, 16)
            return wq.at[pl.ds(at, size), :]
        return wo_all.at[dev, :, pl.ds(pl.multiple_of(start, 128), size)]

    def ring_part(s, dev):
        kind, base, b, a = streams[s]
        return part(kind, dev, base + side * b, a + b)

    def x_part(s, dev, mine):
        kind, base, b, a = streams[s]
        who = side if mine else 1 - side
        return part(kind, dev, base + who * (a + b), b)

    def whole_part(s, dev):
        kind, base, b, a = streams[s]
        return part(kind, dev, base, a + 2 * b)

    def source(d, h, c):
        return chip_at(-h if d == RIGHT else h) * CORES + c

    def remote(ref, send, recv, target, dst=None):
        return pltpu.make_async_remote_copy(
            src_ref=ref, dst_ref=ref if dst is None else dst, send_sem=send,
            recv_sem=recv, device_id=target, device_id_type=MESH,
        )

    def ring_copy(s, d, h):
        return remote(
            ring_part(s, source(d, h - 1, core)), ring_send.at[s, d, h], ring_recv.at[s, d, h],
            to_right if d == RIGHT else to_left,
        )

    def x_copy(s, d, h, mine=True):
        return remote(x_part(s, source(d, h, core), mine), x_send.at[s, d, h], x_recv.at[s, d, h], partner)

    def sib_ring(s, d, h, c):
        return remote(ring_part(s, source(d, h, c)), sa_send.at[s, d, h], sa_recv.at[s, d, h], peer)

    def sib_x(s, d, h, c):
        return remote(x_part(s, source(d, h, c), False), sb_send.at[s, d, h], sb_recv.at[s, d, h], peer)

    def sib_own(s, dev):
        return remote(whole_part(s, dev), own_send.at[s], own_recv.at[s], peer)

    loads = [
        pltpu.make_async_copy(wq_hbm, wq.at[pl.ds(pl.multiple_of(ctx * rows, 16), rows), :], load_sem.at[0]),
        pltpu.make_async_copy(wo_hbm, wo_all.at[ctx], load_sem.at[1]),
        pltpu.make_async_copy(hid_hbm, hid, load_sem.at[2]),
    ]
    for load in loads:
        load.start()

    barrier = pltpu.get_barrier_semaphore()
    for j in range(1, n):
        other = lax.rem(chip + j, n) * CORES + core
        pl.semaphore_signal(barrier, inc=1, device_id=(group, other), device_id_type=MESH)
    pl.semaphore_signal(barrier, inc=1, device_id=peer, device_id_type=MESH)
    if use_x:
        pl.semaphore_signal(barrier, inc=1, device_id=partner, device_id_type=MESH)
    pl.semaphore_wait(barrier, n + (1 if use_x else 0))

    sent = []

    def go(copy):
        copy.start()
        sent.append(copy)

    def start_stream(s):
        for d in (RIGHT, LEFT):
            if hops[s][d] >= 1:
                go(ring_copy(s, d, 1))
        go(sib_own(s, ctx))

    def arrive(s, d, h):
        ring_copy(s, d, h).wait_recv()
        if h + 1 <= hops[s][d]:
            go(ring_copy(s, d, h + 1))
        if use_x and streams[s][2]:
            go(x_copy(s, d, h))
        go(sib_ring(s, d, h, core))

    def arrive_x(s, d, h):
        if use_x and streams[s][2]:
            x_copy(s, d, h, False).wait_recv()
            go(sib_x(s, d, h, core))

    def settle(s, d, h):
        sib_ring(s, d, h, 1 - core).wait_recv()
        if use_x and streams[s][2]:
            sib_x(s, d, h, 1 - core).wait_recv()

    tile = 256 if tokens % 256 == 0 else tokens

    def accumulate(which, first=False):
        at = pl.multiple_of(which * (CORES * rows), 128)
        depth = pl.ds(at, CORES * rows)

        @pl.loop(0, tokens // tile)
        def _(i):
            r = pl.ds(pl.multiple_of(i * tile, tile), tile)
            term = jnp.dot(hid[r, depth], wq[depth, :], preferred_element_type=jnp.float32)
            if first:
                acc[r, :] = term
            else:
                acc[r, :] += term

    def items(pair):
        found = []
        for h in range(1, half + 1):
            for s in pair:
                for d in (RIGHT, LEFT):
                    if h <= hops[s][d]:
                        found.append((s, d, h))
        return found

    loads[0].wait()
    for s in (0, 1):
        start_stream(s)
    loads[1].wait()
    loads[2].wait()
    for s in (0, 1):
        sib_own(s, peer_ctx).wait_recv()
    accumulate(chip, first=True)

    def chip_key(s, d, h):
        return h if d == RIGHT else n - h

    pending = {}
    for s, d, h in items((0, 1)):
        pending.setdefault(chip_key(s, d, h), []).append((s, d, h))

    queue = items((0, 1))
    settled = {}
    lag_x, lag_sum = 2, 5
    length = len(queue)
    for i in range(length + lag_sum):
        if i < length:
            if i == length - 2:
                for s in (2, 3):
                    start_stream(s)
            arrive(*queue[i])
        if 0 <= i - lag_x < length:
            arrive_x(*queue[i - lag_x])
        if 0 <= i - lag_sum < length:
            item = queue[i - lag_sum]
            settle(*item)
            key = chip_key(*item)
            settled[key] = settled.get(key, 0) + 1
            if settled[key] == len(pending[key]):
                accumulate(chip_at(-key))

    o_queue = items((2, 3))
    o_lag = 2
    o_state = [0]

    def o_steps(count):
        for _ in range(count):
            i = o_state[0]
            if i < len(o_queue):
                arrive(*o_queue[i])
            if 0 <= i - o_lag < len(o_queue):
                arrive_x(*o_queue[i - o_lag])
            o_state[0] = i + 1

    o_steps(4)
    proj[...] = acc[...].astype(jnp.bfloat16)

    def cols(kind, h):
        at = kind * width + h * head_size
        return slice(at, at + head_size)

    for h in range(heads):
        st_mine[h] = lax.dot_general(
            proj[:, cols(1, h)], proj[:, cols(2, h)], (((0,), (0,)), ((), ())),
            preferred_element_type=jnp.float32,
        )
    state_copy = remote(st_mine, t_send.at[0], t_recv.at[0], peer, st_peer)
    go(state_copy)

    share = heads // CORES

    def intra(h):
        for i in range(tokens // tile):
            r = slice(i * tile, (i + 1) * tile)
            upto = slice(0, (i + 1) * tile)
            scores = lax.dot_general(
                proj[r, cols(0, h)], proj[upto, cols(1, h)], (((1,), (1,)), ((), ())),
                preferred_element_type=jnp.float32,
            )
            row = lax.broadcasted_iota(jnp.int32, scores.shape, 0) + i * tile
            col = lax.broadcasted_iota(jnp.int32, scores.shape, 1)
            scores = jnp.where(row >= col, scores, 0.0).astype(jnp.bfloat16)
            acc[r, h * head_size : (h + 1) * head_size] = jnp.dot(
                scores, proj[upto, cols(2, h)], preferred_element_type=jnp.float32
            )

    state_copy.wait_recv()
    mine = pl.ds(core * share, share)
    st_out[...] = (st_mine[mine] + st_peer[mine]).astype(st_out.dtype)

    def state_to(j):
        target = lax.rem(chip + j, n) * CORES + core
        return remote(st_out, p_send.at[j], p_recv.at[j], (group, target), st_in.at[j])

    for j in range(1, n):
        @pl.when(chip + j < n)
        def _():
            state_to(j).start()

    o_steps(2)
    intra(0)
    o_steps(2)
    for h in range(1, heads):
        intra(h)

    st_half[...] = jnp.zeros_like(st_half)
    for j in range(1, n):
        @pl.when(chip >= j)
        def _():
            state_to(j).wait_recv()
            st_half[...] += st_in[j].astype(jnp.float32)

    half_copy = remote(st_half, t_send.at[1], t_recv.at[1], peer, st_other)
    go(half_copy)
    o_steps(2)
    half_copy.wait_recv()

    after = core.astype(jnp.float32)
    for h in range(heads):
        own = (h // share) == core
        low = st_half[h % share]
        high = st_other[h % share]
        prior = inc_ref[h] + jnp.where(own, low, high) + after * st_peer[h]
        top = prior.astype(jnp.bfloat16)
        rest = (prior - top.astype(jnp.float32)).astype(jnp.bfloat16)
        o = slice(h * head_size, (h + 1) * head_size)
        for i in range(tokens // tile):
            r = slice(i * tile, (i + 1) * tile)
            query = proj[r, cols(0, h)]
            mixed = (
                acc[r, o]
                + jnp.dot(query, top, preferred_element_type=jnp.float32)
                + jnp.dot(query, rest, preferred_element_type=jnp.float32)
            )
            scale = lax.rsqrt(jnp.mean(mixed * mixed, axis=-1, keepdims=True) + 1e-06)
            normed_ref[r, o] = (mixed * scale * gain_ref[:, o]).astype(jnp.bfloat16)

    o_steps(len(o_queue) + o_lag - o_state[0])
    for s in (2, 3):
        sib_own(s, peer_ctx).wait_recv()
    for item in o_queue:
        settle(*item)
    for copy in sent:
        copy.wait_send()
    for j in range(1, n):
        @pl.when(chip + j < n)
        def _():
            state_to(j).wait_send()


def local(n_groups, n_ctx, hidden, w_qkv, w_out, norm_gain, incoming):
    tokens, model = hidden.shape
    rows, three = w_qkv.shape
    heads, head_size, _ = incoming.shape
    width = three // 3
    out_rows, out_cols = w_out.shape
    fine = w_out.reshape(16, out_rows * out_cols // 16)
    o_cols = fine.shape[1]
    n = n_ctx // CORES
    half = n // 2
    share = heads // CORES
    dma = pltpu.SemaphoreType.DMA
    state = (heads, head_size, head_size)
    part = (share, head_size, head_size)
    flops = 2 * tokens * model * three
    normed, w_all = pl.pallas_call(
        functools.partial(kernel, n_groups, n_ctx, heads, head_size, rows, o_cols),
        out_shape=(
            jax.ShapeDtypeStruct((tokens, width), jnp.bfloat16),
            jax.ShapeDtypeStruct((n_ctx, 16, o_cols), jnp.bfloat16),
        ),
        in_specs=[pl.BlockSpec(memory_space=pl.ANY)] * 3
        + [pl.BlockSpec(memory_space=pltpu.VMEM)] * 2,
        out_specs=(
            pl.BlockSpec(memory_space=pltpu.VMEM),
            pl.BlockSpec(memory_space=pl.ANY),
        ),
        scratch_shapes=[
            pltpu.VMEM((tokens, model), jnp.bfloat16),
            pltpu.VMEM((model, three), jnp.bfloat16),
            pltpu.VMEM((tokens, three), jnp.float32),
            pltpu.VMEM((tokens, three), jnp.bfloat16),
            pltpu.VMEM(state, jnp.float32),
            pltpu.VMEM(state, jnp.float32),
            pltpu.VMEM(part, jnp.bfloat16),
            pltpu.VMEM((n,) + part, jnp.bfloat16),
            pltpu.VMEM(part, jnp.float32),
            pltpu.VMEM(part, jnp.float32),
            dma((3,)),
        ]
        + [dma((4, 2, half + 1))] * 8
        + [dma((4,)), dma((4,)), dma((2,)), dma((2,)), dma((n,)), dma((n,))],
        compiler_params=pltpu.CompilerParams(
            collective_id=0, has_side_effects=True, vmem_limit_bytes=48 * 1024 * 1024
        ),
        cost_estimate=pl.CostEstimate(
            flops=flops, bytes_accessed=tokens * model * 2, transcendentals=0
        ),
    )(hidden, w_qkv, fine, norm_gain.reshape(1, width), incoming)
    w_full = w_all.reshape(n_ctx * out_rows, out_cols)
    result = jnp.dot(normed, w_full, preferred_element_type=jnp.float32)
    return result.astype(jnp.bfloat16)


def solution(mesh):
    body = functools.partial(local, mesh.shape["groups"], mesh.shape["ctx"])
    return jax.shard_map(
        body,
        mesh=mesh,
        in_specs=(
            P(("groups", "ctx"), None),
            P("ctx", None),
            P("ctx", None),
            P(),
            P("groups", None, None),
        ),
        out_specs=P(("groups", "ctx"), None),
        check_vma=False,
    )
```

time: 180 us -> 70.4 us (0.39)
  waiting for transfers between devices: 133 us -> 0 us
  Pallas kernels: 0 us -> 62 us
  other arithmetic: 14.6 us -> 0 us
  matrix products: 18.3 us -> 4.51 us
  between operations: 13.2 us -> 0.01 us
  local copies, waits for them, and re-layouts: 0.09 us -> 3.48 us
    all_gather x3 -> x0, waiting for transfers between devices: 132 us -> none  [the longest x1 66.9 us: local(): lax.all_gather(w_qkv, 'ctx', axis=0, tiled=True)]
    pallas_call x0 -> x1, Pallas kernels: none -> 62 us  [local(): pl.pallas_call(functools.partial(kernel, n_groups, n_ctx, heads, head_siz...]
    select_n x15 -> x0, other arithmetic: 14.3 us -> none  [turn(): return jnp.where(position < mine, longer, running)]
    dot_general x5 -> x1, matrix products: 18.3 us -> 4.51 us  [local(): result = jnp.dot(normed, w_full, preferred_element_type=jnp.float32)]
    unnamed x4 -> x8, local copies, waits for them, and re-layouts: 0.01 us -> 3.48 us
  transfers between devices with their start and end apart: 3 -> 0, of which waited for: 3 -> 0; matrix products, arithmetic and copies ran while one was open for 9% -> 0% of each run, Pallas kernels for 0% -> 0%
where the time goes in v1:
time: 70.4 us; the launch traced here: 70 us
  Pallas kernels  62 us (88%)
  matrix products  4.51 us (6%)
  local copies, waits for them, and re-layouts  3.48 us (5%)
    pallas_call x1, Pallas kernels, local(): pl.pallas_call(functools.partial(kernel, n_groups, n_ctx, heads, head_siz...  62 us
    dot_general x1, matrix products, local(): result = jnp.dot(normed, w_full, preferred_element_type=jnp.float32)  4.51 us
    unnamed x8, local copies, waits for them, and re-layouts  3.48 us

profile of v1, /device:TPU:0, one launch (start us, length us, event | category | flops | bytes accessed | tf_op | source)
XLA Modules:
  0.0 70.0 jit_solution(8557287218847108370)
XLA Ops:
  0.0 0.0 copy-start
  0.0 1.0 %copy-done = bf16[256,768]{1,0:T(8,128)(2,1)S(1)} copy-done((bf16[256,768]{1,0:T(8,128)(2,1)S(1)}, bf16[256,768]{1,0:T(8,128)(2,1)}, u32[]{:S(2)}) %copy-start) | copy-done | bytes 393240
  1.0 0.0 copy-start.1
  1.0 0.9 %copy-done.1 = bf16[16,4096]{1,0:T(8,128)(2,1)S(1)} copy-done((bf16[16,4096]{1,0:T(8,128)(2,1)S(1)}, bf16[16,4096]{1,0:T(8,128)(2,1)}, u32[]{:S(2)}) %copy-start.1) | copy-done | bytes 131096
  1.9 0.0 copy-start.2
  1.9 0.9 %copy-done.2 = f32[2,128,128]{2,1,0:T(8,128)S(1)} copy-done((f32[2,128,128]{2,1,0:T(8,128)S(1)}, f32[2,128,128]{2,1,0:T(8,128)}, u32[]{:S(2)}) %copy-start.2) | copy-done | bytes 131096
  2.8 0.0 copy-start.3
  2.8 0.7 copy-done.3
  3.5 62.0 %shard_map.55 = (bf16[768,256]{1,0:T(8,128)(2,1)S(1)}, bf16[16,16,4096]{2,1,0:T(8,128)(2,1)S(1)}) custom-call(bf16[768,4096]{1,0:T(8,128)(2,1)} %hid_hbm.1, bf16[256,768]{1,0:T(8,128)(2,1)S(1)} %copy-done, bf16[16,4096]{1,0:T(8,128)(2,1)S(1)} %copy-done.1, f32[1,256]{1,0:T(1,128)S(1)} %bitcast.5, f32[2,128,128]{2,1,0:T(8,128)S(1)} %copy-done.2), custom_call_target="tpu_custom_call" | custom-call | flops 4831838208 | bytes 6291456 | tf_op jit(solution)/shard_map/pallas_call | solution.py:355
  65.5 4.5 %convolution_convert_fusion = bf16[768,4096]{1,0:T(8,128)(2,1)} fusion(bf16[768,256]{1,0:T(8,128)(2,1)S(1)} %get-tuple-element.7, bf16[256,4096]{1,0:T(8,128)(2,1)S(1)} %bitcast.4), kind=kOutput, calls=%fused_computation | convolution fusion | flops 1613758464 | bytes 8781824 | tf_op jit(solution)/shard_map/dot_general | solution.py:390
Async XLA Ops:
  0.0 1.0 %copy-start = (bf16[256,768]{1,0:T(8,128)(2,1)S(1)}, bf16[256,768]{1,0:T(8,128)(2,1)}, u32[]{:S(2)}) copy-start(bf16[256,768]{1,0:T(8,128)(2,1)} %wq_hbm.1) | copy-start | bytes 1179652
  1.0 0.9 %copy-start.1 = (bf16[16,4096]{1,0:T(8,128)(2,1)S(1)}, bf16[16,4096]{1,0:T(8,128)(2,1)}, u32[]{:S(2)}) copy-start(bf16[16,4096]{1,0:T(8,128)(2,1)} %wo_hbm.1) | copy-start | bytes 393220
  1.9 0.9 %copy-start.2 = (f32[2,128,128]{2,1,0:T(8,128)S(1)}, f32[2,128,128]{2,1,0:T(8,128)}, u32[]{:S(2)}) copy-start(f32[2,128,128]{2,1,0:T(8,128)} %inc_ref.1) | copy-start | bytes 393220
  2.8 0.7 copy-start.3

commit v2 on v1

--- a/solution.py
+++ b/solution.py
@@ -10,19 +10,23 @@
 MESH = pl.DeviceIdType.MESH
 CORES = 2
 RIGHT, LEFT = 0, 1
-
-
-def bands(units, first):
-    third = units * 5 // 16 if first else -(-units * 5 // 16)
-    return third, units - 2 * third
+LAG_X, LAG_SUM = 12, 22
+
+
+def shares(units, count):
+    if units == 16 and count == 4:
+        return [(1, 1), (1, 1), (2, 1), (1, 3)]
+    sizes = [units * (i + 1) // count - units * i // count for i in range(count)]
+    outer = [min((5 * size + (15 if i % 2 else 0)) // 16, size // 2) for i, size in enumerate(sizes)]
+    return [(b, size - 2 * b) for b, size in zip(outer, sizes)]
 
 
 def kernel(
     n_groups, n_ctx, heads, head_size, rows, o_cols,
-    hid_hbm, wq_hbm, wo_hbm, gain_ref, inc_ref,
+    hid_hbm, wq_hbm, wo_hbm, gain_hbm, inc_hbm,
     normed_ref, wo_all,
-    hid, wq, acc, proj, st_mine, st_peer, st_out, st_in, st_half, st_other,
-    load_sem, ring_send, ring_recv, x_send, x_recv, sa_send, sa_recv, sb_send, sb_recv,
+    hid, wq, gain_ref, inc_ref, acc, proj, st_mine, st_peer, st_out, st_in, st_half, st_other,
+    load_sem, ring_send, ring_recv, x_send, x_recv, sa_send, sa_recv,
     own_send, own_recv, t_send, t_recv, p_send, p_recv,
 ):
     n = n_ctx // CORES
@@ -62,23 +66,27 @@
     to_left = (group, chip_at(-1) * CORES + core)
 
     streams = []
-    q_units = rows // 16 // 2
-    o_units = o_cols // 128 // 2
-    for u in range(2):
-        b, a = bands(q_units, u == 0)
-        streams.append((0, u * q_units * 16, b * 16, a * 16))
-    for u in range(2):
-        b, a = bands(o_units, u == 0)
-        streams.append((1, u * o_units * 128, b * 128, a * 128))
+
+    def cut(kind, unit, pairs):
+        base = 0
+        for b, a in pairs:
+            streams.append((kind, base * unit, b * unit, a * unit))
+            base += 2 * b + a
+
+    row_units, col_units = rows // 16, o_cols // 128
+    cut(0, 16, shares(row_units, 4))
+    cut(1, 16, shares(row_units, 2))
+    cut(2, 128, shares(col_units, 2))
     use_x = n_groups % 2 == 0
     if not use_x:
         streams = [(k, base, 0, 2 * b + a) for k, base, b, a in streams]
-    hops = [(half, n - 1 - half), (n - 1 - half, half)] * 2
+    count = len(streams)
+    hops = [(half, n - 1 - half), (n - 1 - half, half)] * (count // 2)
 
     def part(kind, dev, start, size):
-        if kind == 0:
+        if kind < 2:
             at = pl.multiple_of(dev * rows + start, 16)
-            return wq.at[pl.ds(at, size), :]
+            return wq.at[pl.ds(at, size), width : 3 * width] if kind == 0 else wq.at[pl.ds(at, size), 0:width]
         return wo_all.at[dev, :, pl.ds(pl.multiple_of(start, 128), size)]
 
     def ring_part(s, dev):
@@ -112,11 +120,8 @@
     def x_copy(s, d, h, mine=True):
         return remote(x_part(s, source(d, h, core), mine), x_send.at[s, d, h], x_recv.at[s, d, h], partner)
 
-    def sib_ring(s, d, h, c):
-        return remote(ring_part(s, source(d, h, c)), sa_send.at[s, d, h], sa_recv.at[s, d, h], peer)
-
-    def sib_x(s, d, h, c):
-        return remote(x_part(s, source(d, h, c), False), sb_send.at[s, d, h], sb_recv.at[s, d, h], peer)
+    def sib(s, d, h, c):
+        return remote(whole_part(s, source(d, h, c)), sa_send.at[s, d, h], sa_recv.at[s, d, h], peer)
 
     def sib_own(s, dev):
         return remote(whole_part(s, dev), own_send.at[s], own_recv.at[s], peer)
@@ -125,6 +130,8 @@
         pltpu.make_async_copy(wq_hbm, wq.at[pl.ds(pl.multiple_of(ctx * rows, 16), rows), :], load_sem.at[0]),
         pltpu.make_async_copy(wo_hbm, wo_all.at[ctx], load_sem.at[1]),
         pltpu.make_async_copy(hid_hbm, hid, load_sem.at[2]),
+        pltpu.make_async_copy(gain_hbm, gain_ref, load_sem.at[3]),
+        pltpu.make_async_copy(inc_hbm, inc_ref, load_sem.at[4]),
     ]
     for load in loads:
         load.start()
@@ -156,93 +163,92 @@
             go(ring_copy(s, d, h + 1))
         if use_x and streams[s][2]:
             go(x_copy(s, d, h))
-        go(sib_ring(s, d, h, core))
 
     def arrive_x(s, d, h):
         if use_x and streams[s][2]:
             x_copy(s, d, h, False).wait_recv()
-            go(sib_x(s, d, h, core))
+        go(sib(s, d, h, core))
 
     def settle(s, d, h):
-        sib_ring(s, d, h, 1 - core).wait_recv()
-        if use_x and streams[s][2]:
-            sib_x(s, d, h, 1 - core).wait_recv()
+        sib(s, d, h, 1 - core).wait_recv()
 
     tile = 256 if tokens % 256 == 0 else tokens
 
-    def accumulate(which, first=False):
+    kv, qq = slice(width, 3 * width), slice(0, width)
+
+    def accumulate(which, columns, first=False):
         at = pl.multiple_of(which * (CORES * rows), 128)
         depth = pl.ds(at, CORES * rows)
 
         @pl.loop(0, tokens // tile)
         def _(i):
             r = pl.ds(pl.multiple_of(i * tile, tile), tile)
-            term = jnp.dot(hid[r, depth], wq[depth, :], preferred_element_type=jnp.float32)
+            term = jnp.dot(hid[r, depth], wq[depth, columns], preferred_element_type=jnp.float32)
             if first:
-                acc[r, :] = term
+                acc[r, columns] = term
             else:
-                acc[r, :] += term
-
-    def items(pair):
+                acc[r, columns] += term
+
+    def items(which):
         found = []
         for h in range(1, half + 1):
-            for s in pair:
+            for s in which:
                 for d in (RIGHT, LEFT):
                     if h <= hops[s][d]:
                         found.append((s, d, h))
         return found
 
+    early, late = (0, 1, 2, 3), (4, 5, 6, 7)
+    kv_items, late_items = items(early), items(late)
+    queue = kv_items + late_items
+
+    def part_key(s, d, h):
+        return (streams[s][0], h if d == RIGHT else n - h)
+
+    needed = {}
+    for item in queue:
+        needed[part_key(*item)] = needed.get(part_key(*item), 0) + 1
+
+    settled = {}
+
+    def settle_and_sum(item):
+        settle(*item)
+        key = part_key(*item)
+        settled[key] = settled.get(key, 0) + 1
+        if settled[key] == needed[key] and key[0] < 2:
+            accumulate(chip_at(-key[1]), kv if key[0] == 0 else qq)
+
+    position = [0]
+    late_start = len(kv_items) - len(early)
+
+    def step():
+        i = position[0]
+        position[0] = i + 1
+        if late_start <= i < late_start + len(late):
+            start_stream(late[i - late_start])
+        if i < len(queue):
+            arrive(*queue[i])
+        if 0 <= i - LAG_X < len(queue):
+            arrive_x(*queue[i - LAG_X])
+        if 0 <= i - LAG_SUM < len(queue):
+            settle_and_sum(queue[i - LAG_SUM])
+
     loads[0].wait()
-    for s in (0, 1):
-        start_stream(s)
+    start_stream(0)
+    start_stream(1)
     loads[1].wait()
-    loads[2].wait()
-    for s in (0, 1):
+    start_stream(2)
+    start_stream(3)
+    while position[0] < LAG_SUM // 2:
+        step()
+    for load in loads[2:]:
+        load.wait()
+    for s in early:
         sib_own(s, peer_ctx).wait_recv()
-    accumulate(chip, first=True)
-
-    def chip_key(s, d, h):
-        return h if d == RIGHT else n - h
-
-    pending = {}
-    for s, d, h in items((0, 1)):
-        pending.setdefault(chip_key(s, d, h), []).append((s, d, h))
-
-    queue = items((0, 1))
-    settled = {}
-    lag_x, lag_sum = 2, 5
-    length = len(queue)
-    for i in range(length + lag_sum):
-        if i < length:
-            if i == length - 2:
-                for s in (2, 3):
-                    start_stream(s)
-            arrive(*queue[i])
-        if 0 <= i - lag_x < length:
-            arrive_x(*queue[i - lag_x])
-        if 0 <= i - lag_sum < length:
-            item = queue[i - lag_sum]
-            settle(*item)
-            key = chip_key(*item)
-            settled[key] = settled.get(key, 0) + 1
-            if settled[key] == len(pending[key]):
-                accumulate(chip_at(-key))
-
-    o_queue = items((2, 3))
-    o_lag = 2
-    o_state = [0]
-
-    def o_steps(count):
-        for _ in range(count):
-            i = o_state[0]
-            if i < len(o_queue):
-                arrive(*o_queue[i])
-            if 0 <= i - o_lag < len(o_queue):
-                arrive_x(*o_queue[i - o_lag])
-            o_state[0] = i + 1
-
-    o_steps(4)
-    proj[...] = acc[...].astype(jnp.bfloat16)
+    accumulate(chip, kv, first=True)
+    while position[0] < len(kv_items) + LAG_SUM:
+        step()
+    proj[:, kv] = acc[:, kv].astype(jnp.bfloat16)
 
     def cols(kind, h):
         at = kind * width + h * head_size
@@ -273,6 +279,8 @@
                 scores, proj[upto, cols(2, h)], preferred_element_type=jnp.float32
             )
 
+    step()
+    step()
     state_copy.wait_recv()
     mine = pl.ds(core * share, share)
     st_out[...] = (st_mine[mine] + st_peer[mine]).astype(st_out.dtype)
@@ -286,11 +294,11 @@
         def _():
             state_to(j).start()
 
-    o_steps(2)
-    intra(0)
-    o_steps(2)
-    for h in range(1, heads):
-        intra(h)
+    for s in late:
+        sib_own(s, peer_ctx).wait_recv()
+    accumulate(chip, qq, first=True)
+    while position[0] < len(queue) + LAG_SUM:
+        step()
 
     st_half[...] = jnp.zeros_like(st_half)
     for j in range(1, n):
@@ -301,7 +309,9 @@
 
     half_copy = remote(st_half, t_send.at[1], t_recv.at[1], peer, st_other)
     go(half_copy)
-    o_steps(2)
+    proj[:, qq] = acc[:, qq].astype(jnp.bfloat16)
+    for h in range(heads):
+        intra(h)
     half_copy.wait_recv()
 
     after = core.astype(jnp.float32)
@@ -324,17 +334,16 @@
             scale = lax.rsqrt(jnp.mean(mixed * mixed, axis=-1, keepdims=True) + 1e-06)
             normed_ref[r, o] = (mixed * scale * gain_ref[:, o]).astype(jnp.bfloat16)
 
-    o_steps(len(o_queue) + o_lag - o_state[0])
-    for s in (2, 3):
-        sib_own(s, peer_ctx).wait_recv()
-    for item in o_queue:
-        settle(*item)
     for copy in sent:
         copy.wait_send()
     for j in range(1, n):
         @pl.when(chip + j < n)
         def _():
             state_to(j).wait_send()
+
+
+def project(x_ref, w_ref, o_ref):
+    o_ref[...] = jnp.dot(x_ref[...], w_ref[...], preferred_element_type=jnp.float32).astype(o_ref.dtype)
 
 
 def local(n_groups, n_ctx, hidden, w_qkv, w_out, norm_gain, incoming):
@@ -358,8 +367,7 @@
             jax.ShapeDtypeStruct((tokens, width), jnp.bfloat16),
             jax.ShapeDtypeStruct((n_ctx, 16, o_cols), jnp.bfloat16),
         ),
-        in_specs=[pl.BlockSpec(memory_space=pl.ANY)] * 3
-        + [pl.BlockSpec(memory_space=pltpu.VMEM)] * 2,
+        in_specs=[pl.BlockSpec(memory_space=pltpu.HBM)] * 5,
         out_specs=(
             pl.BlockSpec(memory_space=pltpu.VMEM),
             pl.BlockSpec(memory_space=pl.ANY),
@@ -367,6 +375,8 @@
         scratch_shapes=[
             pltpu.VMEM((tokens, model), jnp.bfloat16),
             pltpu.VMEM((model, three), jnp.bfloat16),
+            pltpu.VMEM((1, width), jnp.float32),
+            pltpu.VMEM(state, jnp.float32),
             pltpu.VMEM((tokens, three), jnp.float32),
             pltpu.VMEM((tokens, three), jnp.bfloat16),
             pltpu.VMEM(state, jnp.float32),
@@ -375,10 +385,10 @@
             pltpu.VMEM((n,) + part, jnp.bfloat16),
             pltpu.VMEM(part, jnp.float32),
             pltpu.VMEM(part, jnp.float32),
-            dma((3,)),
+            dma((5,)),
         ]
-        + [dma((4, 2, half + 1))] * 8
-        + [dma((4,)), dma((4,)), dma((2,)), dma((2,)), dma((n,)), dma((n,))],
+        + [dma((8, 2, half + 1))] * 6
+        + [dma((8,)), dma((8,)), dma((2,)), dma((2,)), dma((n,)), dma((n,))],
         compiler_params=pltpu.CompilerParams(
             collective_id=0, has_side_effects=True, vmem_limit_bytes=48 * 1024 * 1024
         ),
@@ -387,8 +397,21 @@
         ),
     )(hidden, w_qkv, fine, norm_gain.reshape(1, width), incoming)
     w_full = w_all.reshape(n_ctx * out_rows, out_cols)
-    result = jnp.dot(normed, w_full, preferred_element_type=jnp.float32)
-    return result.astype(jnp.bfloat16)
+    block = 256 if tokens % 256 == 0 else tokens
+    return pl.pallas_call(
+        project,
+        grid=(tokens // block,),
+        out_shape=jax.ShapeDtypeStruct((tokens, out_cols), jnp.bfloat16),
+        in_specs=[
+            pl.BlockSpec((block, width), lambda i: (i, 0)),
+            pl.BlockSpec((width, out_cols), lambda i: (0, 0)),
+        ],
+        out_specs=pl.BlockSpec((block, out_cols), lambda i: (i, 0)),
+        compiler_params=pltpu.CompilerParams(vmem_limit_bytes=32 * 1024 * 1024),
+        cost_estimate=pl.CostEstimate(
+            flops=2 * tokens * width * out_cols, bytes_accessed=2 * tokens * out_cols, transcendentals=0
+        ),
+    )(normed, w_full)
 
 
 def solution(mesh):

time: 70.4 us -> 58.4 us (0.83)
  Pallas kernels: 62 us -> 54.7 us
  matrix products: 4.51 us -> 0 us
    pallas_call x1, Pallas kernels: 62 us -> 50.6 us  [local(): pl.pallas_call(functools.partial(kernel, n_groups, n_ctx, heads, head_siz...]
    dot_general x1 -> x0, matrix products: 4.51 us -> none  [local(): result = jnp.dot(normed, w_full, preferred_element_type=jnp.float32)]
    pallas_call x0 -> x1, Pallas kernels: none -> 4.09 us  [local(): pl.pallas_call(project, grid=(tokens // block,), out_shape=jax.ShapeDtype...]
where the time goes in v2:
time: 58.4 us; the launch traced here: 58.2 us
  Pallas kernels  54.7 us (94%)
  local copies, waits for them, and re-layouts  3.48 us (6%)
    pallas_call x1, Pallas kernels, local(): pl.pallas_call(functools.partial(kernel, n_groups, n_ctx, heads, head_siz...  50.6 us
    pallas_call x1, Pallas kernels, local(): pl.pallas_call(project, grid=(tokens // block,), out_shape=jax.ShapeDtype...  4.09 us
    unnamed x8, local copies, waits for them, and re-layouts  3.48 us

profile of v2, /device:TPU:0, one launch (start us, length us, event | category | flops | bytes accessed | tf_op | source)
XLA Modules:
  0.0 58.2 jit_solution(16322347716793295061)
XLA Ops:
  0.0 0.0 copy-start
  0.0 1.0 %copy-done = bf16[256,768]{1,0:T(8,128)(2,1)S(1)} copy-done((bf16[256,768]{1,0:T(8,128)(2,1)S(1)}, bf16[256,768]{1,0:T(8,128)(2,1)}, u32[]{:S(2)}) %copy-start) | copy-done | bytes 393240
  1.0 0.0 copy-start.1
  1.0 0.9 %copy-done.1 = bf16[16,4096]{1,0:T(8,128)(2,1)S(1)} copy-done((bf16[16,4096]{1,0:T(8,128)(2,1)S(1)}, bf16[16,4096]{1,0:T(8,128)(2,1)}, u32[]{:S(2)}) %copy-start.1) | copy-done | bytes 131096
  1.9 0.0 copy-start.2
  1.9 0.9 %copy-done.2 = f32[2,128,128]{2,1,0:T(8,128)S(1)} copy-done((f32[2,128,128]{2,1,0:T(8,128)S(1)}, f32[2,128,128]{2,1,0:T(8,128)}, u32[]{:S(2)}) %copy-start.2) | copy-done | bytes 131096
  2.8 0.0 copy-start.3
  2.8 0.7 %copy-done.3 = f32[256]{0:T(256)S(1)} copy-done((f32[256]{0:T(256)S(1)}, f32[256]{0:T(256)}, u32[]{:S(2)}) %copy-start.3) | copy-done | bytes 1048
  3.5 50.6 %shard_map.55 = (bf16[768,256]{1,0:T(8,128)(2,1)S(1)}, bf16[16,16,4096]{2,1,0:T(8,128)(2,1)S(1)}) custom-call(bf16[768,4096]{1,0:T(8,128)(2,1)} %hid_hbm.1, bf16[256,768]{1,0:T(8,128)(2,1)S(1)} %copy-done, bf16[16,4096]{1,0:T(8,128)(2,1)S(1)} %copy-done.1, f32[1,256]{1,0:T(1,128)S(1)} %bitcast.3, f32[2,128,128]{2,1,0:T(8,128)S(1)} %copy-done.2), custom_call_target="tpu_custom_call" | custom-call | flops 4831838208 | bytes 6291456 | tf_op jit(solution)/shard_map/pallas_call | solution.py:364
  54.1 4.1 %shard_map.56 = bf16[768,4096]{1,0:T(8,128)(2,1)} custom-call(bf16[768,256]{1,0:T(8,128)(2,1)S(1)} %get-tuple-element.7.x_ref, bf16[256,4096]{1,0:T(8,128)(2,1)S(1)} %bitcast.2), custom_call_target="tpu_custom_call" | custom-call | flops 1610612736 | bytes 6291456 | tf_op jit(solution)/shard_map/pallas_call | solution.py:401
Async XLA Ops:
  0.0 1.0 %copy-start = (bf16[256,768]{1,0:T(8,128)(2,1)S(1)}, bf16[256,768]{1,0:T(8,128)(2,1)}, u32[]{:S(2)}) copy-start(bf16[256,768]{1,0:T(8,128)(2,1)} %wq_hbm.1) | copy-start | bytes 1179652
  1.0 0.9 %copy-start.1 = (bf16[16,4096]{1,0:T(8,128)(2,1)S(1)}, bf16[16,4096]{1,0:T(8,128)(2,1)}, u32[]{:S(2)}) copy-start(bf16[16,4096]{1,0:T(8,128)(2,1)} %wo_hbm.1) | copy-start | bytes 393220
  1.9 0.9 %copy-start.2 = (f32[2,128,128]{2,1,0:T(8,128)S(1)}, f32[2,128,128]{2,1,0:T(8,128)}, u32[]{:S(2)}) copy-start(f32[2,128,128]{2,1,0:T(8,128)} %inc_hbm.1) | copy-start | bytes 393220
  2.8 0.7 %copy-start.3 = (f32[256]{0:T(256)S(1)}, f32[256]{0:T(256)}, u32[]{:S(2)}) copy-start(f32[256]{0:T(256)} %param.8) | copy-start | bytes 3076
